TPU v7x, 128 devices: a whole 4x4x4 slice. The times are simulated.
128 devices in a mesh: row: 16 (over z, x), col: 8 (over y, core).
Axes of the slice: x: 4, y: 4, z: 4, core: 2. Of those that a mesh axis runs over, the one named last changes fastest.
Arguments:
- integrals: float32 [12800, 3200], P('row', 'col'), may hold values from -0.109375 to 0.109375
- amplitudes: float32 [8, 40, 400, 400], P('col', None, 'row'), may hold values from -6 to 6
Outputs:
- residual: float32 [12800, 16000], P('row', 'col')
All inputs are finite; a program needn't handle non-finite values.
Results may differ from a plain program's by a relative error of at most 0.00007.
Values sent between devices are 32-bit elements; how exact they have to be, the bound alone decides.
No kernel may reach another device: no remote copies, remote signals or barrier semaphores. Data moves between devices by JAX's collectives and lax.ppermute only.
A program may use at most 192 MiB of HBM per device.

v0:
```python
import jax
import jax.numpy as jnp
from jax import lax
from jax.sharding import PartitionSpec as P


def per_device(integrals, amplitudes):
    rows_here = lax.axis_size("row")
    cols_here = lax.axis_size("col")
    k_here, occupied, b_here, virtual = amplitudes.shape
    j_block = occupied // cols_here
    c_block = virtual // rows_here
    k_total = k_here * cols_here
    panels = lax.all_gather(integrals, "col", axis=1, tiled=True)
    pieces = amplitudes.reshape(k_here, cols_here, j_block, b_here, rows_here, c_block)
    pieces = jnp.transpose(pieces, (4, 1, 0, 2, 3, 5)).reshape(rows_here, cols_here, -1)
    flat_send = pieces.reshape(rows_here * cols_here, -1)
    arrived = lax.all_to_all(flat_send, ("row", "col"), split_axis=0, concat_axis=0, tiled=True)
    arrived = arrived.reshape(rows_here, cols_here, k_here, j_block, b_here, c_block)
    regridded = jnp.transpose(arrived, (5, 1, 2, 3, 0, 4)).reshape(
        c_block * k_total, j_block * virtual
    )
    return jnp.dot(
        panels,
        lax.all_gather(regridded, "row", axis=0, tiled=True),
        precision=lax.Precision.HIGHEST,
        preferred_element_type=jnp.float32,
    )


def solution(mesh):
    return jax.shard_map(
        per_device,
        mesh=mesh,
        in_specs=(P("row", "col"), P("col", None, "row", None)),
        out_specs=P("row", "col"),
        check_vma=False,
    )
```

profile of v0, /device:TPU:8, one launch (start us, length us, event | category | flops | bytes accessed | tf_op | source)
XLA Modules:
  0.0 357.8 jit_solution(1896445747526498132)
XLA Ops:
  6.5 0.0 all-gather.3.cloned.1.call-start
  6.5 0.7 all-gather.3.cloned.1.call-update
  7.3 0.0 all-gather.5.cloned.1.call-start
  7.3 7.8 %reshape.13 = f32[1,8,5,25,16,25]{5,4,2,1,3,0:T(8,128)} reshape(f32[1,40,25,400]{3,1,2,0:T(8,128)} %param.3) | data formatting | bytes 3200000 | tf_op jit(solution)/shard_map/reshape | solution.py:15
  15.1 12.3 %copy.9 = f32[1,8,5,25,16,25]{5,3,2,1,4,0:T(8,128)} copy(f32[1,8,5,25,16,25]{5,4,2,1,3,0:T(8,128)} %reshape.13) | data formatting | bytes 3200000 | tf_op jit(solution)/shard_map/reshape | solution.py:15
  27.4 9.5 %all_to_all.8 = f32[128,1,3125]{2,1,0:T(1,128)S(1)} reshape(f32[16,8,1,5,25,25]{5,4,3,1,0,2:T(8,128)} %bitcast.16) | data formatting | bytes 3200000 | tf_op jit(solution)/shard_map/all_to_all | solution.py:18
  36.9 36.9 %all_to_all.10 = f32[128,1,3125]{2,1,0:T(1,128)S(1)} all-to-all(f32[128,1,3125]{2,1,0:T(1,128)S(1)} %all_to_all.8), channel_id=1, replica_groups=mesh['row'=16,'col'=8] {'row','col'}, dimensions={0} | all-to-all | bytes 3200000 | tf_op jit(solution)/shard_map/all_to_all | solution.py:18
  73.7 3.9 %reduce = f32[128,3125]{1,0:T(8,128)S(1)} reduce(f32[128,1,3125]{2,1,0:T(1,128)S(1)} %all_to_all.10, f32[]{:T(128)} %constant.1), dimensions={1}, to_apply=%all_to_all.7.reduce_sub_computation | reduce | bytes 3200004 | tf_op jit(solution)/shard_map/all_to_all | solution.py:18
  77.6 10.9 %reshape.14 = f32[16,8,1,5,25,25]{5,4,3,1,0,2:T(8,128)} reshape(f32[128,3125]{1,0:T(8,128)S(1)} %reduce) | data formatting | bytes 3200000 | tf_op jit(solution)/shard_map/reshape | solution.py:19
  88.5 11.4 %copy.7 = f32[25,8,1,5,16,25]{5,4,3,1,0,2:T(8,128)} copy(f32[25,8,1,5,16,25]{0,5,3,1,4,2:T(8,128)} %bitcast.17) | data formatting | bytes 3200000 | tf_op jit(solution)/shard_map/transpose | solution.py:20
  99.9 6.7 %reshape.15 = f32[200,2000]{1,0:T(8,128)} reshape(f32[25,8,1,5,16,25]{5,4,3,1,0,2:T(8,128)} %copy.7) | data formatting | bytes 3200000 | tf_op jit(solution)/shard_map/reshape | solution.py:20
  106.6 0.0 all-gather.5.cloned.1.call-update
  106.6 0.0 all-gather.3.cloned.1.call-done
  106.7 158.4 %all-gather.5.cloned.1.call-done = f32[3200,2000]{1,0:T(8,128)} async-done(((f32[200,2000]{1,0:T(8,128)}), f32[3200,2000]{1,0:T(8,128)}) %all-gather.5.cloned.1.call-update) | async-done | bytes 25600016 | tf_op jit(solution)/shard_map/all_gather | solution.py:25
  265.0 86.0 %fusion = f32[800,2000]{1,0:T(8,128)} fusion(f32[800,3200]{0,1:T(8,128)} %all-gather.3.cloned.1.call-done, f32[3200,2000]{1,0:T(8,128)} %all-gather.5.cloned.1.call-done), kind=kOutput, calls=%fused_computation.1 | convolution fusion | flops 61440000000 | bytes 42240000 | tf_op jit(solution)/shard_map/dot_general | solution.py:23
Async XLA Ops:
  6.5 100.1 %all-gather.3.cloned.1.call-start = ((), (), s32[]{:S(2)}) async-start(), calls=%async_computation.1 | async-start | bytes 12902400 | tf_op jit(solution)/shard_map/all_gather | solution.py:14
  7.3 257.8 %all-gather.5.cloned.1.call-start = ((), (), s32[]{:S(2)}) async-start(), calls=%async_computation.2 | async-start | bytes 27852800 | tf_op jit(solution)/shard_map/all_gather | solution.py:25
Sparse Core Ops, SparseCore 0:
  9.0 81.8 all-gather.2
  106.7 158.2 all-gather.4
where the time goes:
time: 359 us; the launch traced here: 358 us
  waiting for transfers between devices  159 us (44%)
  matrix products  86 us (24%)
  local copies, waits for them, and re-layouts  58.5 us (16%)
  blocking collectives  36.9 us (10%)
  between operations  13.4 us (4%)
  other arithmetic  3.9 us (1%)
    all_gather x1, waiting for transfers between devices, per_device(): lax.all_gather(regridded, 'row', axis=0, tiled=True)  158 us
    dot_general x1, matrix products, per_device(): jnp.dot(panels, lax.all_gather(regridded, 'row', axis=0, tiled=True), pre...  86 us
    all_to_all x1, blocking collectives, per_device(): lax.all_to_all(flat_send, ('row', 'col'), split_axis=0, concat_axis=0, ti...  36.9 us
    reshape x2, local copies, waits for them, and re-layouts, per_device(): amplitudes.reshape(k_here, cols_here, j_block, b_here, rows_here, c_block)  20.1 us
    transpose x1, local copies, waits for them, and re-layouts, per_device(): jnp.transpose(arrived, (5, 1, 2, 3, 0, 4))  11.4 us
    reshape x1, local copies, waits for them, and re-layouts, per_device(): arrived.reshape(rows_here, cols_here, k_here, j_block, b_here, c_block)  10.9 us
    all_to_all x1, local copies, waits for them, and re-layouts, per_device(): lax.all_to_all(flat_send, ('row', 'col'), split_axis=0, concat_axis=0, ti...  9.46 us
  transfers between devices with their start and end apart: 2, of which 1 were waited for; matrix products, arithmetic and copies ran while one was open for 15% of the time, Pallas kernels for 0%

commit v1 on v0

v1 whole, which is shorter than its diff:
```python
import functools

import jax
import jax.numpy as jnp
from jax import lax
from jax.experimental import pallas as pl
from jax.experimental.pallas import tpu as pltpu
from jax.sharding import PartitionSpec as P

Z, X, Y, CORES = 4, 4, 4, 2
AXES = ("row", "col")
LANES = 128


def permutation(move):
    pairs = []
    for z in range(Z):
        for x in range(X):
            for y in range(Y):
                for core in range(CORES):
                    to_z, to_x, to_y, to_core = move(z, x, y, core)
                    source = ((z * X + x) * Y + y) * CORES + core
                    target = (((to_z % Z) * X + to_x % X) * Y + to_y % Y) * CORES + to_core
                    pairs.append((source, target))
    return pairs


def send_y(value, distance):
    return lax.ppermute(value, AXES, permutation(lambda z, x, y, core: (z, x, y + distance, core)))


def send_core(value):
    return lax.ppermute(value, AXES, permutation(lambda z, x, y, core: (z, x, y, 1 - core)))


def send_first(value, distance):
    return lax.ppermute(
        value,
        AXES,
        permutation(lambda z, x, y, core: (z + distance * core, x + distance * (1 - core), y, core)),
    )


def send_second(value, distance):
    return lax.ppermute(
        value,
        AXES,
        permutation(lambda z, x, y, core: (z + distance * (1 - core), x + distance * core, y, core)),
    )


def regrid_kernel(j_block, place_ref, amp_ref, out_ref, rows):
    b_here, occupied, virtual = amp_ref.shape
    rows[...] = jnp.zeros_like(rows)
    for q in range(occupied // j_block):
        for j in range(j_block):
            rows[j * b_here : (j + 1) * b_here, :virtual] = amp_ref[:, q * j_block + j, :]
        out_ref[place_ref[q]] = rows[...].T[:virtual]


def regrid(amp, places, j_block):
    b_here, occupied, virtual = amp.shape
    blocks = occupied // j_block
    padded = pl.cdiv(virtual, LANES) * LANES
    return pl.pallas_call(
        functools.partial(regrid_kernel, j_block),
        out_shape=jax.ShapeDtypeStruct((blocks, virtual, LANES), jnp.float32),
        in_specs=[
            pl.BlockSpec(memory_space=pltpu.SMEM),
            pl.BlockSpec(memory_space=pltpu.VMEM),
        ],
        out_specs=pl.BlockSpec(memory_space=pltpu.VMEM),
        scratch_shapes=[pltpu.VMEM((LANES, padded), jnp.float32)],
        compiler_params=pltpu.CompilerParams(vmem_limit_bytes=32 * 2**20),
        name="regrid",
    )(places, amp)


def split(value):
    high = value.astype(jnp.bfloat16)
    low = (value - high.astype(jnp.float32)).astype(jnp.bfloat16)
    return high, low


def panel_kernel(k_total, slot_ref, panel_ref, high_ref, low_ref, ordered):
    depth = panel_ref.shape[0]
    virtual = depth // k_total
    for k in range(k_total):
        start = pl.multiple_of(slot_ref[k] * virtual, 8)
        ordered[pl.ds(start, virtual), :] = panel_ref[pl.ds(k, virtual, stride=k_total), :]
    high_ref[...], low_ref[...] = split(ordered[...].T)


def panels_by_k(panel, slots, k_total):
    depth, rows = panel.shape
    return pl.pallas_call(
        functools.partial(panel_kernel, k_total),
        out_shape=[jax.ShapeDtypeStruct((rows, depth), jnp.bfloat16)] * 2,
        grid=(pl.cdiv(rows, LANES),),
        in_specs=[
            pl.BlockSpec(memory_space=pltpu.SMEM),
            pl.BlockSpec((depth, LANES), lambda i: (0, i)),
        ],
        out_specs=[pl.BlockSpec((LANES, depth), lambda i: (i, 0))] * 2,
        scratch_shapes=[pltpu.VMEM((depth, LANES), jnp.float32)],
        compiler_params=pltpu.CompilerParams(vmem_limit_bytes=32 * 2**20),
        name="panels",
    )(slots, panel)


def product_kernel(pieces, *refs):
    high_ref, low_ref = refs[:2]
    piece_refs = refs[2 : 2 + pieces]
    out_ref, total = refs[2 + pieces :]
    step = pl.program_id(0)

    @pl.when(step == 0)
    def _():
        total[...] = jnp.zeros_like(total)

    high, low = split(jnp.concatenate([ref[...] for ref in piece_refs], axis=1))
    dot = functools.partial(jnp.dot, preferred_element_type=jnp.float32)
    total[...] += dot(high_ref[...], high) + (dot(high_ref[...], low) + dot(low_ref[...], high))

    @pl.when(step == pl.num_programs(0) - 1)
    def _():
        for i in range(pieces):
            out_ref[i] = total[:, i * LANES : (i + 1) * LANES]


def product(high, low, pieces, depth_block=640):
    rows, depth = high.shape
    n = len(pieces)
    return pl.pallas_call(
        functools.partial(product_kernel, n),
        out_shape=jax.ShapeDtypeStruct((n, rows, LANES), jnp.float32),
        grid=(depth // depth_block,),
        in_specs=[pl.BlockSpec((rows, depth_block), lambda i: (0, i))] * 2
        + [pl.BlockSpec((depth_block, LANES), lambda i: (i, 0))] * n,
        out_specs=pl.BlockSpec((n, rows, LANES), lambda i: (0, 0, 0)),
        scratch_shapes=[pltpu.VMEM((rows, n * LANES), jnp.float32)],
        compiler_params=pltpu.CompilerParams(vmem_limit_bytes=40 * 2**20),
        cost_estimate=pl.CostEstimate(
            flops=6 * rows * depth * n * LANES,
            bytes_accessed=4 * depth * (rows + n * LANES),
            transcendentals=0,
        ),
        name="product",
    )(high, low, *pieces)


def order_kernel(j_block, b_here, places_ref, *refs):
    *group_refs, out_ref, by_row = refs
    slot = 0
    for ref in group_refs:
        for i in range(ref.shape[0]):
            by_row[places_ref[slot]] = ref[i]
            slot += 1
    rows, width = out_ref.shape
    blocks = by_row.shape[0]
    virtual = blocks * b_here
    lane = lax.broadcasted_iota(jnp.int32, (rows, LANES), 1)
    for tile in range(pl.cdiv(width, LANES)):
        first = tile * LANES
        last = min(first + LANES, width)
        value = jnp.zeros((rows, LANES), jnp.float32)
        for j in range(j_block):
            for block in range(blocks):
                start = j * virtual + block * b_here
                if start >= last or start + b_here <= first:
                    continue
                moved = pltpu.roll(by_row[block], (start - first - j * b_here) % LANES, 1)
                inside = (lane >= start - first) & (lane < start - first + b_here)
                value = jnp.where(inside, moved, value)
        out_ref[:, first:last] = value[:, : last - first]


def order(groups, places, j_block, b_here, row_block=80):
    blocks = sum(group.shape[0] for group in groups)
    rows = groups[0].shape[1]
    width = blocks * b_here * j_block
    return pl.pallas_call(
        functools.partial(order_kernel, j_block, b_here),
        out_shape=jax.ShapeDtypeStruct((rows, width), jnp.float32),
        grid=(rows // row_block,),
        in_specs=[pl.BlockSpec(memory_space=pltpu.SMEM)]
        + [pl.BlockSpec((g.shape[0], row_block, LANES), lambda i: (0, i, 0)) for g in groups],
        out_specs=pl.BlockSpec((row_block, width), lambda i: (i, 0)),
        scratch_shapes=[pltpu.VMEM((blocks, row_block, LANES), jnp.float32)],
        compiler_params=pltpu.CompilerParams(vmem_limit_bytes=32 * 2**20),
        name="order",
    )(places, *groups)


def per_device(integrals, amplitudes):
    rows_here = lax.axis_size("row")
    cols_here = lax.axis_size("col")
    k_here, occupied, b_here, virtual = amplitudes.shape
    j_block = occupied // cols_here
    k_total = k_here * cols_here
    row, col = lax.axis_index("row"), lax.axis_index("col")
    z, x, y, core = row // X, row % X, col // CORES, col % CORES

    panel = lax.all_gather(integrals.T, "col", axis=0, tiled=True)

    q = jnp.arange(cols_here, dtype=jnp.int32)
    away = (q // CORES - y) % Y
    other = (q % CORES) ^ core
    kept = regrid(amplitudes[0].transpose(1, 0, 2), other * Y + away, j_block)
    kept, given = kept[:Y], kept[Y:]
    pairs = jnp.concatenate([kept, send_core(given)], axis=1)
    own = jnp.concatenate(
        [pairs[0], send_y(pairs[1], 1), send_y(pairs[3], -1), send_y(pairs[2], 2)], axis=0
    )

    before = send_first(own, 1)
    after = send_first(own, -1)
    half = own.shape[0] // 2
    across = jnp.concatenate([send_first(before[:half], 1), send_first(after[half:], -1)], axis=0)
    line = [own, before, after, across]
    line_offset = [0, -1, 1, 2]
    second_before = [send_second(piece, 1) for piece in line]
    second_after = [send_second(piece, -1) for piece in line]
    second_across = [
        send_second(second_before[i], 1) if i % 2 == 0 else send_second(second_after[i], -1)
        for i in range(4)
    ]

    slot_of_away = jnp.array([0, 1, 3, 2], jnp.int32)
    k = jnp.arange(k_total, dtype=jnp.int32)
    slots = 2 * slot_of_away[(y - k // CORES) % Y] + ((k % CORES) ^ core)
    high, low = panels_by_k(panel, slots, k_total)

    grouped = [
        [(line[i], line_offset[i], 0) for i in range(4)],
        [(s[i], line_offset[i], d) for i in (0, 1) for s, d in ((second_before, -1), (second_after, 1))],
        [(s[i], line_offset[i], d) for i in (2, 3) for s, d in ((second_before, -1), (second_after, 1))],
        [(second_across[i], line_offset[i], 2) for i in range(4)],
    ]
    products, places = [], []
    for group in grouped:
        products.append(product(high, low, [piece for piece, _, _ in group]))
        for _, first, second in group:
            from_core0 = ((z + second) % Z) * X + (x + first) % X
            from_core1 = ((z + first) % Z) * X + (x + second) % X
            places.append(jnp.where(core == 0, from_core0, from_core1))
    return order(products, jnp.stack(places).astype(jnp.int32), j_block, b_here)


def solution(mesh):
    return jax.shard_map(
        per_device,
        mesh=mesh,
        in_specs=(P("row", "col"), P("col", None, "row", None)),
        out_specs=P("row", "col"),
        check_vma=False,
    )
```

time: 359 us -> 247 us (0.69)
  matrix products: 86 us -> 0 us
  Pallas kernels: 0 us -> 74.1 us
  waiting for transfers between devices: 159 us -> 104 us
  local copies, waits for them, and re-layouts: 58.5 us -> 18.2 us
  blocking collectives: 36.9 us -> 0 us
  starting transfers between devices: 0.04 us -> 36.6 us
  other arithmetic: 3.9 us -> 0.26 us
    all_gather x2 -> x1, waiting for transfers between devices: 158 us -> 0.01 us  [per_device(): panel = lax.all_gather(integrals.T, 'col', axis=0, tiled=True)]
    ppermute x0 -> x20, waiting for transfers between devices: none -> 103 us  [the longest x4 45.7 us: send_first(): lax.ppermute(value, AXES, permutation(lambda z, x, y, core: (z + distance...]
    dot_general x1 -> x0, matrix products: 86 us -> none  [per_device(): jnp.dot(panels, lax.all_gather(regridded, 'row', axis=0, tiled=True), pre...]
    pallas_call x0 -> x7, Pallas kernels: none -> 74.1 us  [the longest x4 50.4 us: product(): pl.pallas_call(functools.partial(product_kernel, n), out_shape=jax.ShapeD...]
    reshape x4 -> x0, local copies, waits for them, and re-layouts: 37.7 us -> none  [the longest x2 20.1 us: per_device(): amplitudes.reshape(k_here, cols_here, j_block, b_here, rows_here, c_block)]
    all_to_all x1 -> x0, blocking collectives: 36.9 us -> none  [per_device(): lax.all_to_all(flat_send, ('row', 'col'), split_axis=0, concat_axis=0, ti...]
    ppermute x0 -> x20, starting transfers between devices: none -> 36.6 us  [the longest x12 25.2 us: send_second(): lax.ppermute(value, AXES, permutation(lambda z, x, y, core: (z + distance...]
    unnamed x0 -> x21, local copies, waits for them, and re-layouts: none -> 15.1 us
  transfers between devices with their start and end apart: 2 -> 21, of which waited for: 1 -> 9; matrix products, arithmetic and copies ran while one was open for 15% -> 2% of each run, Pallas kernels for 0% -> 20%
where the time goes in v1:
time: 247 us
  waiting for transfers between devices  104 us (42%)
  Pallas kernels  74.1 us (30%)
  starting transfers between devices  36.6 us (15%)
  local copies, waits for them, and re-layouts  18.2 us (7%)
  between operations  13.6 us (6%)
    pallas_call x4, Pallas kernels, product(): pl.pallas_call(functools.partial(product_kernel, n), out_shape=jax.ShapeD...  50.4 us
    ppermute x4, waiting for transfers between devices, send_first(): lax.ppermute(value, AXES, permutation(lambda z, x, y, core: (z + distance...  45.7 us
    ppermute x3, waiting for transfers between devices, send_y(): lax.ppermute(value, AXES, permutation(lambda z, x, y, core: (z, x, y + di...  29.7 us
    ppermute x12, waiting for transfers between devices, send_second(): lax.ppermute(value, AXES, permutation(lambda z, x, y, core: (z + distance...  25.4 us
    ppermute x12, starting transfers between devices, send_second(): lax.ppermute(value, AXES, permutation(lambda z, x, y, core: (z + distance...  25.2 us
    unnamed x21, local copies, waits for them, and re-layouts  15.1 us
    pallas_call x1, Pallas kernels, order(): pl.pallas_call(functools.partial(order_kernel, j_block, b_here), out_shap...  13.1 us
    pallas_call x1, Pallas kernels, panels_by_k(): pl.pallas_call(functools.partial(panel_kernel, k_total), out_shape=[jax.S...  9.18 us
  transfers between devices with their start and end apart: 21, of which 9 were waited for; matrix products, arithmetic and copies ran while one was open for 2% of the time, Pallas kernels for 20%

profile of v1, /device:TPU:8, one launch (start us, length us, event | category | flops | bytes accessed | tf_op | source)
XLA Modules:
  0.0 246.6 jit_solution(15875282866332718253)
XLA Ops:
  7.3 1.6 copy-done.1
  8.9 1.4 regrid.1
  10.5 2.3 collective-permute-done
  13.0 2.4 collective-permute-start.3
  15.3 1.3 collective-permute-start.2
  17.4 10.1 %collective-permute-done.3 = f32[800,128]{1,0:T(8,128)S(1)} collective-permute-done((f32[800,128]{1,0:T(8,128)S(1)}, f32[800,128]{1,0:T(8,128)S(1)}, u32[]{:S(2)}, u32[]{:S(2)}) %collective-permute-start.3) | collective-permute-done | bytes 409632 | tf_op jit(solution)/shard_map/ppermute | solution.py:29
  27.5 16.0 %collective-permute-done.2 = f32[800,128]{1,0:T(8,128)S(1)} collective-permute-done((f32[800,128]{1,0:T(8,128)S(1)}, f32[800,128]{1,0:T(8,128)S(1)}, u32[]{:S(2)}, u32[]{:S(2)}) %collective-permute-start.2) | collective-permute-done | bytes 409632 | tf_op jit(solution)/shard_map/ppermute | solution.py:29
  43.5 3.6 %collective-permute-done.1 = f32[800,128]{1,0:T(8,128)S(1)} collective-permute-done((f32[800,128]{1,0:T(8,128)S(1)}, f32[800,128]{1,0:T(8,128)S(1)}, u32[]{:S(2)}, u32[]{:S(2)}) %collective-permute-start.1) | collective-permute-done | bytes 409632 | tf_op jit(solution)/shard_map/ppermute | solution.py:29
  47.2 1.3 collective-permute-start.4
  48.6 2.0 collective-permute-start.5
  50.5 2.0 collective-permute-start.8
  52.6 2.8 %collective-permute-start.9 = (f32[3200,128]{1,0:T(8,128)S(1)}, f32[3200,128]{1,0:T(8,128)S(1)}, u32[]{:S(2)}, u32[]{:S(2)}) collective-permute-start(f32[3200,128]{1,0:T(8,128)S(1)} %pad_maximum_fusion.refs_2_), channel_id=1, source_target_pairs={{0,96},{1,25},{2,98},{3,27},{4,100},{5,29},{6,102},{7,31},{8,104},... | collective-permute-start | bytes 4915208 | tf_op jit(solution)/shard_map/ppermute | solution.py:45
  55.4 30.2 %collective-permute-done.4.refs_3_ = f32[3200,128]{1,0:T(8,128)S(1)} collective-permute-done((f32[3200,128]{1,0:T(8,128)S(1)}, f32[3200,128]{1,0:T(8,128)S(1)}, u32[]{:S(2)}, u32[]{:S(2)}) %collective-permute-start.4) | collective-permute-done | bytes 1638432 | tf_op jit(solution)/shard_map/ppermute | solution.py:37
  87.0 3.5 %collective-permute-start.7 = (f32[1600,128]{1,0:T(8,128)S(1)}, f32[1600,128]{1,0:T(8,128)S(1)}, u32[]{:S(2)}, u32[]{:S(2)}) collective-permute-start(f32[1600,128]{1,0:T(8,128)S(1)} %slice.43), channel_id=1, source_target_pairs={{0,24},{1,97},{2,26},{3,99},{4,28},{5,101},{6,30},{7,103},{8,0},{9... | collective-permute-start | bytes 2457608 | tf_op jit(solution)/shard_map/ppermute | solution.py:37
  90.5 2.2 collective-permute-start.10
  92.7 15.4 %collective-permute-done.6 = f32[1600,128]{1,0:T(8,128)S(1)} collective-permute-done((f32[1600,128]{1,0:T(8,128)S(1)}, f32[1600,128]{1,0:T(8,128)S(1)}, u32[]{:S(2)}, u32[]{:S(2)}) %collective-permute-start.6) | collective-permute-done | bytes 819232 | tf_op jit(solution)/shard_map/ppermute | solution.py:37
  108.1 5.7 %collective-permute-start.11 = (f32[3200,128]{1,0:T(8,128)S(1)}, f32[3200,128]{1,0:T(8,128)}, u32[]{:S(2)}, u32[]{:S(2)}) collective-permute-start(f32[3200,128]{1,0:T(8,128)S(1)} %collective-permute-done.4.refs_3_), channel_id=1, source_target_pairs={{0,96},{1,25},{2,98},{3,27},{4,100},{5,29},{6,102},{7,31},{8,104},... | collective-permute-start | bytes 4915208 | tf_op jit(solution)/shard_map/ppermute | solution.py:45
  115.8 3.2 %collective-permute-start.13 = (f32[3200,128]{1,0:T(8,128)}, f32[3200,128]{1,0:T(8,128)}, u32[]{:S(2)}, u32[]{:S(2)}) collective-permute-start(f32[3200,128]{1,0:T(8,128)} %collective-permute-done.5.refs_4_), channel_id=1, source_target_pairs={{0,96},{1,25},{2,98},{3,27},{4,100},{5,29},{6,102},{7,31},{8,104},... | collective-permute-start | bytes 4915208 | tf_op jit(solution)/shard_map/ppermute | solution.py:45
  123.2 4.3 %copy-done = f32[3200,800]{1,0:T(8,128)S(1)} copy-done((f32[3200,800]{1,0:T(8,128)S(1)}, f32[3200,800]{1,0:T(8,128)}, u32[]{:S(2)}) %copy-start) | copy-done | bytes 10240024
  127.4 9.2 %panels.1 = (bf16[800,3200]{1,0:T(8,128)(2,1)S(1)}, bf16[800,3200]{1,0:T(8,128)(2,1)S(1)}) custom-call(s32[8]{0:T(128)S(1)} %multiply_add_fusion.slot_ref, f32[3200,800]{1,0:T(8,128)S(1)} %copy-done), custom_call_target="tpu_custom_call" | custom-call | tf_op jit(solution)/shard_map/panels/pallas_call | solution.py:96
  136.6 2.3 copy-done.4
  139.0 3.2 %collective-permute-start.17 = (f32[3200,128]{1,0:T(8,128)}, f32[3200,128]{1,0:T(8,128)}, u32[]{:S(2)}, u32[]{:S(2)}) collective-permute-start(f32[3200,128]{1,0:T(8,128)} %collective-permute-done.11.refs_5_), channel_id=1, source_target_pairs={{0,96},{1,25},{2,98},{3,27},{4,100},{5,29},{6,102},{7,31},{8,104},... | collective-permute-start | bytes 4915208 | tf_op jit(solution)/shard_map/ppermute | solution.py:45
  142.2 8.0 %collective-permute-done.13.refs_3_ = f32[3200,128]{1,0:T(8,128)} collective-permute-done((f32[3200,128]{1,0:T(8,128)}, f32[3200,128]{1,0:T(8,128)}, u32[]{:S(2)}, u32[]{:S(2)}) %collective-permute-start.13) | collective-permute-done | bytes 1638432 | tf_op jit(solution)/shard_map/ppermute | solution.py:45
  150.3 17.4 %collective-permute-done.15.refs_5_ = f32[3200,128]{1,0:T(8,128)} collective-permute-done((f32[3200,128]{1,0:T(8,128)}, f32[3200,128]{1,0:T(8,128)}, u32[]{:S(2)}, u32[]{:S(2)}) %collective-permute-start.15) | collective-permute-done | bytes 1638432 | tf_op jit(solution)/shard_map/ppermute | solution.py:45
  167.7 3.7 %collective-permute-start.19 = (f32[3200,128]{1,0:T(8,128)}, f32[3200,128]{1,0:T(8,128)}, u32[]{:S(2)}, u32[]{:S(2)}) collective-permute-start(f32[3200,128]{1,0:T(8,128)} %collective-permute-done.15.refs_5_), channel_id=1, source_target_pairs={{0,96},{1,25},{2,98},{3,27},{4,100},{5,29},{6,102},{7,31},{8,104},... | collective-permute-start | bytes 4915208 | tf_op jit(solution)/shard_map/ppermute | solution.py:45
  171.4 12.6 %product.4.refs_0_ = f32[4,800,128]{2,1,0:T(8,128)S(1)} custom-call(bf16[800,3200]{1,0:T(8,128)(2,1)S(1)} %get-tuple-element.7.refs_0_, bf16[800,3200]{1,0:T(8,128)(2,1)} %copy-done.4, f32[3200,128]{1,0:T(8,128)S(1)} %pad_maximum_fusion.refs_2_, f32[3200,128]{1,0:T(8,128)S(1)} %collective-permute-done.4.refs_3_, f32[3200,128]{1,0:T(8,128)} %collective-permute-done.5.refs_4_, ...), custom_call_target="tpu_custom_call" | custom-call | flops 7864320000 | bytes 16793600 | tf_op jit(solution)/shard_map/product/pallas_call | solution.py:134
  184.0 2.3 copy-done.2
  186.3 2.4 copy-done.3
  188.7 12.5 %product.5.refs_1_ = f32[4,800,128]{2,1,0:T(8,128)S(1)} custom-call(bf16[800,3200]{1,0:T(8,128)(2,1)S(1)} %copy-done.3, bf16[800,3200]{1,0:T(8,128)(2,1)} %copy-done.4, f32[3200,128]{1,0:T(8,128)S(1)} %copy-done.6, f32[3200,128]{1,0:T(8,128)S(1)} %copy-done.8, f32[3200,128]{1,0:T(8,128)} %collective-permute-done.10.refs_4_, ...), custom_call_target="tpu_custom_call" | custom-call | flops 7864320000 | bytes 16793600 | tf_op jit(solution)/shard_map/product/pallas_call | solution.py:134
  201.3 12.7 %product.6.refs_2_ = f32[4,800,128]{2,1,0:T(8,128)S(1)} custom-call(bf16[800,3200]{1,0:T(8,128)(2,1)S(1)} %copy-done.3, bf16[800,3200]{1,0:T(8,128)(2,1)} %copy-done.4, f32[3200,128]{1,0:T(8,128)} %collective-permute-done.12.refs_2_, f32[3200,128]{1,0:T(8,128)} %collective-permute-done.13.refs_3_, f32[3200,128]{1,0:T(8,128)} %collective-permute-done.14.refs_4_, ...), custom_call_target="tpu_custom_call" | custom-call | flops 7864320000 | bytes 16793600 | tf_op jit(solution)/shard_map/product/pallas_call | solution.py:134
  214.0 12.6 %product.7.refs_3_ = f32[4,800,128]{2,1,0:T(8,128)S(1)} custom-call(bf16[800,3200]{1,0:T(8,128)(2,1)S(1)} %copy-done.3, bf16[800,3200]{1,0:T(8,128)(2,1)} %copy-done.4, f32[3200,128]{1,0:T(8,128)S(1)} %collective-permute-done.16.refs_2_, f32[3200,128]{1,0:T(8,128)} %collective-permute-done.17.refs_3_, f32[3200,128]{1,0:T(8,128)} %collective-permute-done.18.refs_4_, ...), custom_call_target="tpu_custom_call" | custom-call | flops 7864320000 | bytes 16793600 | tf_op jit(solution)/shard_map/product/pallas_call | solution.py:134
  226.6 13.1 %order.1 = f32[800,2000]{1,0:T(8,128)} custom-call(s32[16]{0:T(128)S(1)} %stack.67.places_ref, f32[4,800,128]{2,1,0:T(8,128)S(1)} %product.4.refs_0_, f32[4,800,128]{2,1,0:T(8,128)S(1)} %product.5.refs_1_, f32[4,800,128]{2,1,0:T(8,128)S(1)} %product.6.refs_2_, f32[4,800,128]{2,1,0:T(8,128)S(1)} %product.7.refs_3_), custom_call_target="tpu_custom_call" | custom-call | tf_op jit(solution)/shard_map/order/pallas_call | solution.py:182
  (51 shorter events, 9.5 us)
Async XLA Ops:
  6.5 116.6 %all-gather.2.cloned.1.call-start = ((), (), s32[]{:S(2)}) async-start(), calls=%async_computation | async-start | bytes 12902400 | tf_op jit(solution)/shard_map/all_gather | solution.py:204
  7.3 1.6 copy-start.1
  10.4 2.4 collective-permute-start
  13.0 14.5 %collective-permute-start.3 = (f32[800,128]{1,0:T(8,128)S(1)}, f32[800,128]{1,0:T(8,128)S(1)}, u32[]{:S(2)}, u32[]{:S(2)}) collective-permute-start(f32[800,128]{1,0:T(8,128)S(1)} %get-tuple-element.11), channel_id=1, source_target_pairs={{0,4},{1,5},{2,6},{3,7},{4,0},{5,1},{6,2},{7,3},{8,12},{9,13},{10,... | collective-permute-start | bytes 1228808 | tf_op jit(solution)/shard_map/ppermute | solution.py:29
  15.3 28.2 %collective-permute-start.2 = (f32[800,128]{1,0:T(8,128)S(1)}, f32[800,128]{1,0:T(8,128)S(1)}, u32[]{:S(2)}, u32[]{:S(2)}) collective-permute-start(f32[800,128]{1,0:T(8,128)S(1)} %get-tuple-element.12), channel_id=1, source_target_pairs={{0,6},{1,7},{2,0},{3,1},{4,2},{5,3},{6,4},{7,5},{8,14},{9,15},{10,... | collective-permute-start | bytes 1228808 | tf_op jit(solution)/shard_map/ppermute | solution.py:29
  16.7 30.4 %collective-permute-start.1 = (f32[800,128]{1,0:T(8,128)S(1)}, f32[800,128]{1,0:T(8,128)S(1)}, u32[]{:S(2)}, u32[]{:S(2)}) collective-permute-start(f32[800,128]{1,0:T(8,128)S(1)} %get-tuple-element.10), channel_id=1, source_target_pairs={{0,2},{1,3},{2,4},{3,5},{4,6},{5,7},{6,0},{7,1},{8,10},{9,11},{10,... | collective-permute-start | bytes 1228808 | tf_op jit(solution)/shard_map/ppermute | solution.py:29
  47.2 38.4 %collective-permute-start.4 = (f32[3200,128]{1,0:T(8,128)S(1)}, f32[3200,128]{1,0:T(8,128)S(1)}, u32[]{:S(2)}, u32[]{:S(2)}) collective-permute-start(f32[3200,128]{1,0:T(8,128)S(1)} %pad_maximum_fusion.refs_2_), channel_id=1, source_target_pairs={{0,8},{1,33},{2,10},{3,35},{4,12},{5,37},{6,14},{7,39},{8,16},{9,4... | collective-permute-start | bytes 4915208 | tf_op jit(solution)/shard_map/ppermute | solution.py:37
  48.6 37.2 %collective-permute-start.5 = (f32[3200,128]{1,0:T(8,128)S(1)}, f32[3200,128]{1,0:T(8,128)}, u32[]{:S(2)}, u32[]{:S(2)}) collective-permute-start(f32[3200,128]{1,0:T(8,128)S(1)} %pad_maximum_fusion.refs_2_), channel_id=1, source_target_pairs={{0,24},{1,97},{2,26},{3,99},{4,28},{5,101},{6,30},{7,103},{8,0},{9... | collective-permute-start | bytes 4915208 | tf_op jit(solution)/shard_map/ppermute | solution.py:37
  50.5 65.3 %collective-permute-start.8 = (f32[3200,128]{1,0:T(8,128)S(1)}, f32[3200,128]{1,0:T(8,128)S(1)}, u32[]{:S(2)}, u32[]{:S(2)}) collective-permute-start(f32[3200,128]{1,0:T(8,128)S(1)} %pad_maximum_fusion.refs_2_), channel_id=1, source_target_pairs={{0,32},{1,9},{2,34},{3,11},{4,36},{5,13},{6,38},{7,15},{8,40},{9,1... | collective-permute-start | bytes 4915208 | tf_op jit(solution)/shard_map/ppermute | solution.py:45
  52.6 66.5 %collective-permute-start.9 = (f32[3200,128]{1,0:T(8,128)S(1)}, f32[3200,128]{1,0:T(8,128)S(1)}, u32[]{:S(2)}, u32[]{:S(2)}) collective-permute-start(f32[3200,128]{1,0:T(8,128)S(1)} %pad_maximum_fusion.refs_2_), channel_id=1, source_target_pairs={{0,96},{1,25},{2,98},{3,27},{4,100},{5,29},{6,102},{7,31},{8,104},... | collective-permute-start | bytes 4915208 | tf_op jit(solution)/shard_map/ppermute | solution.py:45
  85.6 22.5 %collective-permute-start.6 = (f32[1600,128]{1,0:T(8,128)S(1)}, f32[1600,128]{1,0:T(8,128)S(1)}, u32[]{:S(2)}, u32[]{:S(2)}) collective-permute-start(f32[1600,128]{1,0:T(8,128)S(1)} %slice.42), channel_id=1, source_target_pairs={{0,8},{1,33},{2,10},{3,35},{4,12},{5,37},{6,14},{7,39},{8,16},{9,4... | collective-permute-start | bytes 2457608 | tf_op jit(solution)/shard_map/ppermute | solution.py:37
  87.0 34.4 %copy-start.9 = (s32[4]{0:T(128)S(1)}, s32[4]{0:T(128)}, u32[]{:S(2)}) copy-start(s32[4]{0:T(128)} %constant.240.clone) | copy-start | bytes 52
  87.0 27.8 %collective-permute-start.7 = (f32[1600,128]{1,0:T(8,128)S(1)}, f32[1600,128]{1,0:T(8,128)S(1)}, u32[]{:S(2)}, u32[]{:S(2)}) collective-permute-start(f32[1600,128]{1,0:T(8,128)S(1)} %slice.43), channel_id=1, source_target_pairs={{0,24},{1,97},{2,26},{3,99},{4,28},{5,101},{6,30},{7,103},{8,0},{9... | collective-permute-start | bytes 2457608 | tf_op jit(solution)/shard_map/ppermute | solution.py:37
  90.5 31.7 %collective-permute-start.10 = (f32[3200,128]{1,0:T(8,128)S(1)}, f32[3200,128]{1,0:T(8,128)}, u32[]{:S(2)}, u32[]{:S(2)}) collective-permute-start(f32[3200,128]{1,0:T(8,128)S(1)} %collective-permute-done.4.refs_3_), channel_id=1, source_target_pairs={{0,32},{1,9},{2,34},{3,11},{4,36},{5,13},{6,38},{7,15},{8,40},{9,1... | collective-permute-start | bytes 4915208 | tf_op jit(solution)/shard_map/ppermute | solution.py:45
  108.1 30.8 %collective-permute-start.11 = (f32[3200,128]{1,0:T(8,128)S(1)}, f32[3200,128]{1,0:T(8,128)}, u32[]{:S(2)}, u32[]{:S(2)}) collective-permute-start(f32[3200,128]{1,0:T(8,128)S(1)} %collective-permute-done.4.refs_3_), channel_id=1, source_target_pairs={{0,96},{1,25},{2,98},{3,27},{4,100},{5,29},{6,102},{7,31},{8,104},... | collective-permute-start | bytes 4915208 | tf_op jit(solution)/shard_map/ppermute | solution.py:45
  114.8 24.2 %collective-permute-start.12 = (f32[3200,128]{1,0:T(8,128)}, f32[3200,128]{1,0:T(8,128)}, u32[]{:S(2)}, u32[]{:S(2)}) collective-permute-start(f32[3200,128]{1,0:T(8,128)} %collective-permute-done.5.refs_4_), channel_id=1, source_target_pairs={{0,32},{1,9},{2,34},{3,11},{4,36},{5,13},{6,38},{7,15},{8,40},{9,1... | collective-permute-start | bytes 4915208 | tf_op jit(solution)/shard_map/ppermute | solution.py:45
  115.8 3.2 %copy-start.5 = (f32[3200,128]{1,0:T(8,128)}, f32[3200,128]{1,0:T(8,128)S(1)}, u32[]{:S(2)}) copy-start(f32[3200,128]{1,0:T(8,128)S(1)} %collective-permute-done.8.refs_2_) | copy-start | bytes 4915204
  115.8 34.4 %collective-permute-start.13 = (f32[3200,128]{1,0:T(8,128)}, f32[3200,128]{1,0:T(8,128)}, u32[]{:S(2)}, u32[]{:S(2)}) collective-permute-start(f32[3200,128]{1,0:T(8,128)} %collective-permute-done.5.refs_4_), channel_id=1, source_target_pairs={{0,96},{1,25},{2,98},{3,27},{4,100},{5,29},{6,102},{7,31},{8,104},... | collective-permute-start | bytes 4915208 | tf_op jit(solution)/shard_map/ppermute | solution.py:45
  119.0 1.2 copy-start.7
  120.3 47.5 %collective-permute-start.15 = (f32[3200,128]{1,0:T(8,128)}, f32[3200,128]{1,0:T(8,128)}, u32[]{:S(2)}, u32[]{:S(2)}) collective-permute-start(f32[3200,128]{1,0:T(8,128)} %constant_dynamic-update-slice_fusion.refs_5_), channel_id=1, source_target_pairs={{0,96},{1,25},{2,98},{3,27},{4,100},{5,29},{6,102},{7,31},{8,104},... | collective-permute-start | bytes 4915208 | tf_op jit(solution)/shard_map/ppermute | solution.py:45
  122.2 79.0 %collective-permute-start.14 = (f32[3200,128]{1,0:T(8,128)}, f32[3200,128]{1,0:T(8,128)}, u32[]{:S(2)}, u32[]{:S(2)}) collective-permute-start(f32[3200,128]{1,0:T(8,128)} %constant_dynamic-update-slice_fusion.refs_5_), channel_id=1, source_target_pairs={{0,32},{1,9},{2,34},{3,11},{4,36},{5,13},{6,38},{7,15},{8,40},{9,1... | collective-permute-start | bytes 4915208 | tf_op jit(solution)/shard_map/ppermute | solution.py:45
  123.2 4.3 %copy-start = (f32[3200,800]{1,0:T(8,128)S(1)}, f32[3200,800]{1,0:T(8,128)}, u32[]{:S(2)}) copy-start(f32[3200,800]{1,0:T(8,128)} %all-gather.2.cloned.1.call-done.panel_ref) | copy-start | bytes 30720004
  127.4 11.5 %copy-start.6 = (f32[3200,128]{1,0:T(8,128)S(1)}, f32[3200,128]{1,0:T(8,128)}, u32[]{:S(2)}) copy-start(f32[3200,128]{1,0:T(8,128)} %copy-done.5) | copy-start | bytes 4915204
  136.6 2.3 copy-start.4
  138.9 75.0 %collective-permute-start.16 = (f32[3200,128]{1,0:T(8,128)S(1)}, f32[3200,128]{1,0:T(8,128)S(1)}, u32[]{:S(2)}, u32[]{:S(2)}) collective-permute-start(f32[3200,128]{1,0:T(8,128)S(1)} %copy-done.6), channel_id=1, source_target_pairs={{0,32},{1,9},{2,34},{3,11},{4,36},{5,13},{6,38},{7,15},{8,40},{9,1... | collective-permute-start | bytes 4915208 | tf_op jit(solution)/shard_map/ppermute | solution.py:45
  139.0 74.9 %collective-permute-start.17 = (f32[3200,128]{1,0:T(8,128)}, f32[3200,128]{1,0:T(8,128)}, u32[]{:S(2)}, u32[]{:S(2)}) collective-permute-start(f32[3200,128]{1,0:T(8,128)} %collective-permute-done.11.refs_5_), channel_id=1, source_target_pairs={{0,96},{1,25},{2,98},{3,27},{4,100},{5,29},{6,102},{7,31},{8,104},... | collective-permute-start | bytes 4915208 | tf_op jit(solution)/shard_map/ppermute | solution.py:45
  150.2 63.8 %collective-permute-start.18 = (f32[3200,128]{1,0:T(8,128)}, f32[3200,128]{1,0:T(8,128)}, u32[]{:S(2)}, u32[]{:S(2)}) collective-permute-start(f32[3200,128]{1,0:T(8,128)} %collective-permute-done.12.refs_2_), channel_id=1, source_target_pairs={{0,32},{1,9},{2,34},{3,11},{4,36},{5,13},{6,38},{7,15},{8,40},{9,1... | collective-permute-start | bytes 4915208 | tf_op jit(solution)/shard_map/ppermute | solution.py:45
  167.7 46.3 %collective-permute-start.19 = (f32[3200,128]{1,0:T(8,128)}, f32[3200,128]{1,0:T(8,128)}, u32[]{:S(2)}, u32[]{:S(2)}) collective-permute-start(f32[3200,128]{1,0:T(8,128)} %collective-permute-done.15.refs_5_), channel_id=1, source_target_pairs={{0,96},{1,25},{2,98},{3,27},{4,100},{5,29},{6,102},{7,31},{8,104},... | collective-permute-start | bytes 4915208 | tf_op jit(solution)/shard_map/ppermute | solution.py:45
  171.4 14.9 %copy-start.8 = (f32[3200,128]{1,0:T(8,128)S(1)}, f32[3200,128]{1,0:T(8,128)}, u32[]{:S(2)}) copy-start(f32[3200,128]{1,0:T(8,128)} %copy-done.7) | copy-start | bytes 4915204
  184.0 2.3 copy-start.2
  186.3 2.5 copy-start.3
Sparse Core Ops, SparseCore 0:
  9.0 73.9 all-gather.1
